TPU v7x, 32 devices: a whole 2x2x4 slice. The times are simulated.
32 devices in a mesh: img: 8 (over z, y), row: 4 (over x, core).
Axes of the slice: x: 2, y: 2, z: 4, core: 2. Of those that a mesh axis runs over, the one named last changes fastest.
Arguments:
- images: bfloat16 [24, 32, 32, 384], P('img', 'row'), may hold values from -8 to 8
- level_count: int32 [24], P('img'), may hold values from 2 to 1280
- level_index: int32 [24], P('img'), may hold values from 0 to 1278, as said below
- labels: int32 [24], P('img'), may hold values from 0 to 999
- first_gain: bfloat16 [384], replicated, may hold values from 0.5 to 1.5
- first_shift: bfloat16 [384], replicated, may hold values from -1.75 to 1.75
- first_kernel: bfloat16 [3456, 384], replicated, may hold values from -0.109375 to 0.109375
- first_offset: bfloat16 [384], replicated, may hold values from -1.75 to 1.75
- embed_weight: bfloat16 [768, 768], replicated, may hold values from -0.21875 to 0.21875
- embed_offset: bfloat16 [768], replicated, may hold values from -1.75 to 1.75
- class_table: bfloat16 [1000, 768], replicated, may hold values from -6 to 6
- second_gain: bfloat16 [384], replicated, may hold values from 0.5 to 1.5
- second_shift: bfloat16 [384], replicated, may hold values from -1.75 to 1.75
- second_kernel: bfloat16 [3456, 384], replicated, may hold values from -0.109375 to 0.109375
- second_offset: bfloat16 [384], replicated, may hold values from -1.75 to 1.75
- third_gain: bfloat16 [384], replicated, may hold values from 0.5 to 1.5
- third_shift: bfloat16 [384], replicated, may hold values from -1.75 to 1.75
- joint_weight: bfloat16 [384, 1152], replicated, may hold values from -0.3125 to 0.3125
- joint_offset: bfloat16 [768], replicated, may hold values from -1.75 to 1.75
- output_weight: bfloat16 [384, 384], replicated, may hold values from -2.5 to 2.5
- output_offset: bfloat16 [384], replicated, may hold values from -1.75 to 1.75
- cotangent: bfloat16 [24, 32, 32, 384], P('img', 'row'), may hold values from -8 to 8
Outputs:
- result: bfloat16 [24, 32, 32, 384], P('img', 'row')
- images_gradient: float32 [24, 32, 32, 384], P('img', 'row')
- first_gain_gradient: float32 [384], P('row')
- first_shift_gradient: float32 [384], P('row')
- first_kernel_gradient: float32 [3456, 384], P('row')
- first_offset_gradient: float32 [384], P('row')
- embed_weight_gradient: float32 [768, 768], P('row')
- embed_offset_gradient: float32 [768], P('row')
- class_table_gradient: float32 [1000, 768], P('row')
- second_gain_gradient: float32 [384], P('row')
- second_shift_gradient: float32 [384], P('row')
- second_kernel_gradient: float32 [3456, 384], P('row')
- second_offset_gradient: float32 [384], P('row')
- third_gain_gradient: float32 [384], P('row')
- third_shift_gradient: float32 [384], P('row')
- joint_weight_gradient: float32 [384, 1152], P('row')
- joint_offset_gradient: float32 [768], P('row')
- output_weight_gradient: float32 [384, 384], P('row')
- output_offset_gradient: float32 [384], P('row')
Inputs may be any that keep to these rules, and one draw needn't show every extreme that they name: Each image's level_index is below its level_count - 1.
All inputs are finite; a program needn't handle non-finite values.
Results may differ from a plain program's by a relative error of at most 0.017.
Values may be sent and summed in bfloat16 or wider, within the bound.
A program may use at most 192 MiB of HBM per device.

v0:
```python
import math

import jax
import jax.numpy as jnp
from jax import lax
from jax.sharding import PartitionSpec as P

GROUPS = 32
HEAD = 64
EMB = 768


norm_eps = 1e-05
sigma_least = 0.002
sigma_most = 80.0
sigma_power = 7.0
highest = lax.Precision.HIGHEST
float_type = jnp.float32
low_type = jnp.bfloat16
contract_rows = (((0,), (0,)), ((), ()))
contract_cols = (((1,), (1,)), ((), ()))


def extended(x, sides, width):
    for axis, dim in sides:
        size, length = (lax.axis_size(axis), x.shape[dim])
        up = [(i, (i + 1) % size) for i in range(size - 1)]
        down = [(j, i) for i, j in up]
        last = lax.slice_in_dim(x, length - width, length, axis=dim)
        initial = lax.slice_in_dim(x, 0, width, axis=dim)
        before = lax.ppermute(last, axis, up)
        after = lax.ppermute(initial, axis, down)
        x = jnp.concatenate([before, x, after], axis=dim)
    return x


def noise_features(level_count, level_index):
    position = (level_index.astype(jnp.float32) + 1.0) / (level_count.astype(jnp.float32) - 1.0)
    low_root = sigma_least ** (1.0 / sigma_power)
    high_root = sigma_most ** (1.0 / sigma_power)
    noise_level = (low_root + position * (high_root - low_root)) ** sigma_power
    noise_time = 250.0 * jnp.log(noise_level)
    half_width = EMB // 2
    frequency = jnp.exp(-math.log(10000.0) * jnp.arange(half_width, dtype=jnp.float32) / half_width)
    angles = noise_time[:, None] * frequency[None, :]
    return jnp.concatenate([jnp.cos(angles), jnp.sin(angles)], axis=-1)


def group_stats(values):
    image_count, pixels, channels = values.shape
    grouped = values.reshape(image_count, pixels, GROUPS, channels // GROUPS)
    first_sum = jnp.sum(grouped, axis=(1, 3))
    second_sum = jnp.sum(grouped * grouped, axis=(1, 3))
    first_sum, second_sum = lax.psum((first_sum, second_sum), "row")
    entries = pixels * lax.axis_size("row") * (channels // GROUPS)
    centre = first_sum / entries
    scaled = lax.rsqrt(second_sum / entries - centre * centre + norm_eps)
    return (centre, scaled)


def normalize(values, centre, scaled):
    image_count, pixels, channels = values.shape
    grouped = values.reshape(image_count, pixels, GROUPS, channels // GROUPS)
    return ((grouped - centre[:, None, :, None]) * scaled[:, None, :, None]).reshape(values.shape)


def group_back(upstream, normed, scaled):
    image_count, pixels, channels = upstream.shape
    grouped_up = upstream.reshape(image_count, pixels, GROUPS, channels // GROUPS)
    grouped_norm = normed.reshape(image_count, pixels, GROUPS, channels // GROUPS)
    first_sum = jnp.sum(grouped_up, axis=(1, 3))
    second_sum = jnp.sum(grouped_up * grouped_norm, axis=(1, 3))
    first_sum, second_sum = lax.psum((first_sum, second_sum), "row")
    entries = pixels * lax.axis_size("row") * (channels // GROUPS)
    outcome = scaled[:, None, :, None] * (
        grouped_up
        - first_sum[:, None, :, None] / entries
        - grouped_norm * (second_sum[:, None, :, None] / entries)
    )
    return outcome.reshape(upstream.shape)


def silu_slope(values):
    sigmoid_part = jax.nn.sigmoid(values)
    return sigmoid_part * (1.0 + values * (1.0 - sigmoid_part))


def padded_rows(activity):
    framed = extended(activity, (("row", 1),), 1)
    return jnp.pad(framed, ((0, 0), (0, 0), (1, 1), (0, 0)))


def padded_grads(gradient):
    framed = extended(gradient, (("row", 1),), 1)
    return jnp.pad(framed, ((0, 0), (0, 0), (1, 1), (0, 0)))


def forward_patches(framed, stripe_rows, image_width):
    pieces = [
        framed[:, row_tap : row_tap + stripe_rows, col_tap : col_tap + image_width, :]
        for row_tap in range(3)
        for col_tap in range(3)
    ]
    joined = jnp.concatenate(pieces, axis=-1)
    return joined.reshape(-1, joined.shape[-1])


def backward_patches(framed, stripe_rows, image_width):
    pieces = [
        framed[
            :, 2 - row_tap : 2 - row_tap + stripe_rows, 2 - col_tap : 2 - col_tap + image_width, :
        ]
        for row_tap in range(3)
        for col_tap in range(3)
    ]
    joined = jnp.concatenate(pieces, axis=-1)
    return joined.reshape(-1, joined.shape[-1])


def transpose_product(columns, kernel):
    channels = kernel.shape[1]
    stacked = columns.reshape(columns.shape[0], 9, channels)
    kernel_taps = kernel.reshape(9, kernel.shape[0] // 9, channels)
    return lax.dot_general(
        stacked, kernel_taps, (((1, 2), (0, 2)), ((), ())), preferred_element_type=float_type
    )


def first_half(flattened, centre, scaled, gain_vector, shift_vector, kernel, offset, layout):
    normed_one = normalize(flattened, centre, scaled)
    pre_one = normed_one * gain_vector + shift_vector
    activity = jax.nn.silu(pre_one).astype(low_type)
    framed = padded_rows(activity.reshape(layout))
    columns_one = forward_patches(framed, layout[1], layout[2])
    hidden = (jnp.dot(columns_one, kernel, preferred_element_type=float_type) + offset).reshape(
        flattened.shape
    )
    return (normed_one, pre_one, columns_one, hidden)


def second_half(hidden, centre, scaled, gain_vector, shift_vector, scale_part, shift_part, layout):
    normed_two = normalize(hidden, centre, scaled)
    shaped = normed_two * gain_vector + shift_vector
    pre_two = shaped * (1.0 + scale_part[:, None, :]) + shift_part[:, None, :]
    activity = jax.nn.silu(pre_two).astype(low_type)
    framed = padded_rows(activity.reshape(layout))
    columns_two = forward_patches(framed, layout[1], layout[2])
    return (normed_two, shaped, pre_two, columns_two)


def shards(
    images,
    level_count,
    level_index,
    labels,
    first_gain,
    first_shift,
    first_kernel,
    first_offset,
    embed_weight,
    embed_offset,
    class_table,
    second_gain,
    second_shift,
    second_kernel,
    second_offset,
    third_gain,
    third_shift,
    joint_weight,
    joint_offset,
    output_weight,
    output_offset,
    cotangent,
):
    image_count, stripe_rows, image_width, channels = images.shape
    layout = (image_count, stripe_rows, image_width, channels)
    pixels = stripe_rows * image_width
    head_count = channels // HEAD
    score_scale = HEAD ** (-0.5)
    gain_one = first_gain.astype(float_type)
    shift_one = first_shift.astype(float_type)
    gain_two = second_gain.astype(float_type)
    shift_two = second_shift.astype(float_type)
    gain_three = third_gain.astype(float_type)
    shift_three = third_shift.astype(float_type)
    offset_one = first_offset.astype(float_type)
    offset_two = second_offset.astype(float_type)
    features = noise_features(level_count, level_index)
    class_count = class_table.shape[0]
    one_hot = (labels[:, None] == jnp.arange(class_count, dtype=jnp.int32)[None, :]).astype(
        low_type
    )
    embedded = features + jnp.dot(one_hot, class_table, preferred_element_type=float_type)
    embed_act = jax.nn.silu(embedded).astype(low_type)
    modulate = jnp.dot(
        embed_act, embed_weight, preferred_element_type=float_type
    ) + embed_offset.astype(float_type)
    scale_part = modulate[:, :channels]
    shift_part = modulate[:, channels:]
    flattened = images.astype(float_type).reshape(image_count, pixels, channels)
    centre_one, scaled_one = group_stats(flattened)
    normed_one, pre_one, columns_one, hidden = first_half(
        flattened, centre_one, scaled_one, gain_one, shift_one, first_kernel, offset_one, layout
    )
    centre_two, scaled_two = group_stats(hidden)
    normed_two, shaped, pre_two, columns_two = second_half(
        hidden, centre_two, scaled_two, gain_two, shift_two, scale_part, shift_part, layout
    )
    branch = (
        jnp.dot(columns_two, second_kernel, preferred_element_type=float_type) + offset_two
    ).reshape(image_count, pixels, channels)
    middle = (flattened + branch) * math.sqrt(0.5)
    centre_three, scaled_three = group_stats(middle)
    normed_three = normalize(middle, centre_three, scaled_three)
    attend_input = (
        (normed_three * gain_three + shift_three)
        .astype(low_type)
        .reshape(image_count * pixels, channels)
    )
    zero_part = jnp.zeros((channels,), low_type)
    joint_bias = jnp.concatenate(
        [joint_offset[:channels], zero_part, joint_offset[channels:]]
    ).astype(float_type)
    joint_rows = (
        jnp.dot(attend_input, joint_weight, preferred_element_type=float_type) + joint_bias
    ).astype(low_type)
    joint_rows = joint_rows.reshape(image_count, pixels, 3 * channels)
    query_local = joint_rows[:, :, :channels]
    key_local = joint_rows[:, :, channels : 2 * channels]
    value_local = joint_rows[:, :, 2 * channels :]
    key_rows, value_rows = (
        lax.all_gather(key_local, "row", axis=1, tiled=True),
        lax.all_gather(value_local, "row", axis=1, tiled=True),
    )
    query_heads = query_local.reshape(image_count, pixels, head_count, HEAD)
    key_heads = key_rows.reshape(image_count, -1, head_count, HEAD)
    value_heads = value_rows.reshape(image_count, -1, head_count, HEAD)
    scores = (
        jnp.einsum("iphd,ikhd->ihpk", query_heads, key_heads, preferred_element_type=float_type)
        * score_scale
    )
    row_peak = jnp.max(scores, axis=-1, keepdims=True)
    raised = jnp.exp(scores - row_peak)
    row_total = jnp.sum(raised, axis=-1, keepdims=True)
    weights = raised / row_total
    log_total = row_peak + jnp.log(row_total)
    weights_low = weights.astype(low_type)
    mixed_rows = jnp.einsum(
        "ihpk,ikhd->iphd", weights_low, value_heads, preferred_element_type=float_type
    )
    mixed_rows = mixed_rows.reshape(image_count * pixels, channels).astype(low_type)
    outcome = (
        middle.reshape(image_count * pixels, channels)
        + jnp.dot(mixed_rows, output_weight, preferred_element_type=float_type)
        + output_offset.astype(float_type)
    )
    result = outcome.astype(low_type).reshape(layout)
    cotangent_low = cotangent.reshape(image_count * pixels, channels)
    upstream = cotangent_low.astype(float_type)
    output_weight_grad = lax.dot_general(
        mixed_rows, cotangent_low, contract_rows, preferred_element_type=float_type
    )
    output_offset_grad = jnp.sum(upstream, axis=0)
    mixed_grad = lax.dot_general(
        cotangent_low, output_weight, contract_cols, preferred_element_type=float_type
    )
    mixed_grad = mixed_grad.astype(low_type).reshape(image_count, pixels, head_count, HEAD)
    scores = (
        jnp.einsum("iphd,ikhd->ihpk", query_heads, key_heads, preferred_element_type=float_type)
        * score_scale
    )
    weights = jnp.exp(scores - log_total)
    weights_low = weights.astype(low_type)
    value_part = jnp.einsum(
        "ihpk,iphd->ikhd", weights_low, mixed_grad, preferred_element_type=float_type
    )
    weight_grad = jnp.einsum(
        "iphd,ikhd->ihpk", mixed_grad, value_heads, preferred_element_type=float_type
    )
    row_inner = jnp.sum(weights * weight_grad, axis=-1, keepdims=True)
    score_grad = (weights * (weight_grad - row_inner)).astype(low_type)
    query_grad = (
        jnp.einsum("ihpk,ikhd->iphd", score_grad, key_heads, preferred_element_type=float_type)
        * score_scale
    )
    key_part = (
        jnp.einsum("ihpk,iphd->ikhd", score_grad, query_heads, preferred_element_type=float_type)
        * score_scale
    )
    key_grad, value_grad = (
        lax.psum_scatter(
            key_part.astype(jnp.bfloat16), "row", scatter_dimension=1, tiled=True
        ).astype(jnp.float32),
        lax.psum_scatter(
            value_part.astype(jnp.bfloat16), "row", scatter_dimension=1, tiled=True
        ).astype(jnp.float32),
    )
    joint_grad = jnp.concatenate(
        [
            query_grad.reshape(image_count * pixels, channels),
            key_grad.reshape(image_count * pixels, channels),
            value_grad.reshape(image_count * pixels, channels),
        ],
        axis=-1,
    ).astype(low_type)
    joint_grad_wide = joint_grad.astype(float_type)
    joint_offset_grad = jnp.concatenate(
        [
            jnp.sum(joint_grad_wide[:, :channels], axis=0),
            jnp.sum(joint_grad_wide[:, 2 * channels :], axis=0),
        ]
    )
    joint_weight_grad = lax.dot_general(
        attend_input, joint_grad, contract_rows, preferred_element_type=float_type
    )
    attend_grad = lax.dot_general(
        joint_grad, joint_weight, contract_cols, preferred_element_type=float_type
    )
    attend_grad = attend_grad.reshape(image_count, pixels, channels)
    third_gain_grad = jnp.sum(attend_grad * normed_three, axis=(0, 1))
    third_shift_grad = jnp.sum(attend_grad, axis=(0, 1))
    middle_grad = upstream.reshape(image_count, pixels, channels) + group_back(
        attend_grad * gain_three, normed_three, scaled_three
    )
    normed_one, pre_one, columns_one, hidden = first_half(
        flattened, centre_one, scaled_one, gain_one, shift_one, first_kernel, offset_one, layout
    )
    normed_two, shaped, pre_two, columns_two = second_half(
        hidden, centre_two, scaled_two, gain_two, shift_two, scale_part, shift_part, layout
    )
    skip_grad = middle_grad * math.sqrt(0.5)
    branch_grad = skip_grad.reshape(image_count * pixels, channels).astype(low_type)
    second_offset_grad = jnp.sum(branch_grad.astype(float_type), axis=0)
    second_kernel_grad = lax.dot_general(
        columns_two, branch_grad, contract_rows, preferred_element_type=float_type
    )
    framed_two = padded_grads(branch_grad.reshape(layout))
    act_two_grad = transpose_product(
        backward_patches(framed_two, stripe_rows, image_width), second_kernel
    )
    pre_two_grad = act_two_grad.reshape(image_count, pixels, channels) * silu_slope(pre_two)
    scale_grad = jnp.sum(pre_two_grad * shaped, axis=1)
    shift_grad = jnp.sum(pre_two_grad, axis=1)
    modulate_grad = jnp.concatenate([scale_grad, shift_grad], axis=-1)
    shaped_grad = pre_two_grad * (1.0 + scale_part[:, None, :])
    second_gain_grad = jnp.sum(shaped_grad * normed_two, axis=(0, 1))
    second_shift_grad = jnp.sum(shaped_grad, axis=(0, 1))
    hidden_grad = group_back(shaped_grad * gain_two, normed_two, scaled_two)
    hidden_grad = hidden_grad.reshape(image_count * pixels, channels).astype(low_type)
    first_offset_grad = jnp.sum(hidden_grad.astype(float_type), axis=0)
    first_kernel_grad = lax.dot_general(
        columns_one, hidden_grad, contract_rows, preferred_element_type=float_type
    )
    framed_one = padded_grads(hidden_grad.reshape(layout))
    act_one_grad = transpose_product(
        backward_patches(framed_one, stripe_rows, image_width), first_kernel
    )
    pre_one_grad = act_one_grad.reshape(image_count, pixels, channels) * silu_slope(pre_one)
    first_gain_grad = jnp.sum(pre_one_grad * normed_one, axis=(0, 1))
    first_shift_grad = jnp.sum(pre_one_grad, axis=(0, 1))
    images_gradient = skip_grad + group_back(pre_one_grad * gain_one, normed_one, scaled_one)
    images_gradient = images_gradient.reshape(layout)
    embed_weight_grad = lax.dot_general(
        embed_act.astype(float_type), modulate_grad, contract_rows, precision=highest
    )
    embed_offset_grad = jnp.sum(modulate_grad, axis=0)
    active_grad = lax.dot_general(
        modulate_grad, embed_weight.astype(float_type), contract_cols, precision=highest
    )
    embedded_grad = active_grad * silu_slope(embedded)
    class_table_grad = lax.dot_general(
        one_hot.astype(float_type), embedded_grad, contract_rows, precision=highest
    )
    summed = lax.psum(
        (
            first_gain_grad,
            first_shift_grad,
            first_kernel_grad,
            first_offset_grad,
            embed_weight_grad,
            embed_offset_grad,
            class_table_grad,
            second_gain_grad,
            second_shift_grad,
            second_kernel_grad,
            second_offset_grad,
            third_gain_grad,
            third_shift_grad,
            joint_weight_grad,
            joint_offset_grad,
            output_weight_grad,
            output_offset_grad,
        ),
        ("img", "row"),
    )
    stripe_index = lax.axis_index("row")
    stripe_count = lax.axis_size("row")
    gradients = tuple(
        (
            lax.dynamic_slice_in_dim(
                item_value,
                stripe_index * (item_value.shape[0] // stripe_count),
                item_value.shape[0] // stripe_count,
                0,
            )
            for item_value in summed
        )
    )
    return (result, images_gradient) + tuple(gradients)


def solution(mesh):
    in_specs = (
        P("img", "row", None, None),
        P("img"),
        P("img"),
        P("img"),
        P(),
        P(),
        P(),
        P(),
        P(),
        P(),
        P(),
        P(),
        P(),
        P(),
        P(),
        P(),
        P(),
        P(),
        P(),
        P(),
        P(),
        P("img", "row", None, None),
    )
    out_specs = (
        P("img", "row", None, None),
        P("img", "row", None, None),
        P("row"),
        P("row"),
        P("row", None),
        P("row"),
        P("row", None),
        P("row"),
        P("row", None),
        P("row"),
        P("row"),
        P("row", None),
        P("row"),
        P("row"),
        P("row"),
        P("row", None),
        P("row"),
        P("row", None),
        P("row"),
    )
    return jax.shard_map(shards, mesh=mesh, in_specs=in_specs, out_specs=out_specs, check_vma=False)
```

profile of v0, /device:TPU:0, one launch (start us, length us, event | category | flops | bytes accessed | tf_op | source)
XLA Modules:
  0.0 686.9 jit_solution(10782237551207886472)
XLA Ops:
  10.5 8.3 %all-reduce.11 = (f32[3,32]{1,0:T(4,128)S(1)}, f32[3,32]{1,0:T(4,128)S(1)}) all-reduce(f32[3,32]{1,0:T(4,128)S(1)} %reduce_sum.313, f32[3,32]{1,0:T(4,128)S(1)} %reduce_sum.310), channel_id=1, replica_groups=mesh['img'=8,'row'=4] {'row'}, use_global_device_ids=true, to_apply=%region_5.6 | all-reduce | flops 192 | bytes 1536 | tf_op jit(solution)/shard_map/psum | solution.py:54
  32.8 4.0 convolution_add_fusion.3
  44.2 5.6 all-reduce.10
  64.9 7.6 %all-reduce.9 = (f32[3,32]{1,0:T(4,128)S(1)}, f32[3,32]{1,0:T(4,128)S(1)}) all-reduce(f32[3,32]{1,0:T(4,128)S(1)} %reduce_sum.321, f32[3,32]{1,0:T(4,128)S(1)} %reduce_sum.318), channel_id=1, replica_groups=mesh['img'=8,'row'=4] {'row'}, use_global_device_ids=true, to_apply=%region_15.16 | all-reduce | flops 192 | bytes 1536 | tf_op jit(solution)/shard_map/psum | solution.py:54
  89.8 15.1 %all-gather.5.cloned.1.call-done = bf16[3,1024,384]{2,1,0:T(8,128)(2,1)} async-done(((bf16[3,256,384]{2,1,0:T(8,128)(2,1)}), bf16[3,1024,384]{2,1,0:T(8,128)(2,1)}) %all-gather.5.cloned.1.call-update) | async-done | bytes 2359312 | tf_op jit(solution)/shard_map/all_gather | solution.py:232
  104.9 4.3 copy.143
  109.2 11.8 %multiply_reduce_fusion.1 = (f32[3,6,256]{2,1,0:T(8,128)}, f32[3,6,256,1024]{3,2,1,0:T(8,128)}) fusion(bf16[3,256,6,64]{1,3,2,0:T(8,128)(2,1)} %bitcast.273, bf16[3,1024,6,64]{1,3,2,0:T(8,128)(2,1)} %bitcast.247), kind=kOutput, calls=%fused_computation.6 | convolution fusion | flops 613412352 | bytes 21841920 | tf_op jit(solution)/shard_map/iphd,ikhd->ihpk/dot_general | solution.py:239
  121.0 10.4 %fusion = f32[3,6,256]{2,1,0:T(8,128)} fusion(f32[3,6,256,1024]{3,2,1,0:T(8,128)} %get-tuple-element.103, f32[3,6,256]{2,1,0:T(8,128)} %get-tuple-element.102), kind=kLoop, calls=%fused_computation.5 | loop fusion | flops 14151168 | bytes 18911232 | tf_op jit(solution)/shard_map/reduce_sum | solution.py:244
  132.8 4.3 copy.141
  137.1 13.7 %multiply_reduce_fusion = (f32[3,6,256]{2,1,0:T(8,128)S(1)}, f32[3,6,256,1024]{3,2,1,0:T(8,128)}) fusion(f32[3,6,256,1024]{3,2,1,0:T(8,128)} %get-tuple-element.103, f32[3,6,256]{2,1,0:T(8,128)} %log_add_fusion, bf16[3,256,6,64]{1,3,2,0:T(8,128)(2,1)} %copy.146, bf16[3,1024,6,64]{1,3,2,0:T(8,128)(2,1)} %bitcast.267), kind=kOutput, calls=%fused_computation.1 | convolution fusion | flops 622849536 | bytes 40734720 | tf_op jit(solution)/shard_map/iphd,ikhd->ihpk/dot_general | solution.py:277
  150.8 13.5 %multiply_convert_fusion = bf16[3,6,256,1024]{3,2,1,0:T(8,128)(2,1)S(1)} fusion(f32[3,6,256,1024]{3,2,1,0:T(8,128)} %get-tuple-element.105, f32[3,6,256,1024]{3,2,1,0:T(8,128)} %get-tuple-element.103, f32[3,6,256]{2,1,0:T(8,128)S(1)} %get-tuple-element.104, f32[3,6,256]{2,1,0:T(8,128)S(1)} %copy-done.23), kind=kLoop, calls=%fused_computation | loop fusion | flops 23592960 | bytes 47222784 | tf_op jit(solution)/shard_map/convert_element_type | solution.py:281
  164.4 3.7 copy-done.1
  171.3 11.7 %convert_bitcast_fusion = bf16[3,1024,6,64]{1,3,2,0:T(8,128)(2,1)} fusion(bf16[3,256,6,64]{1,3,2,0:T(8,128)(2,1)} %copy.146, f32[3,6,256,1024]{3,2,1,0:T(8,128)} %get-tuple-element.103, f32[3,6,256]{2,1,0:T(8,128)} %log_add_fusion), kind=kOutput, calls=%fused_computation.22 | convolution fusion | flops 619315200 | bytes 21841920 | tf_op jit(solution)/shard_map/ihpk,iphd->ikhd/dot_general | solution.py:274
  187.5 5.1 reshape.313
  213.1 10.4 %fusion.33 = bf16[3,256,6,64]{1,3,2,0:T(8,128)(2,1)S(1)} fusion(bf16[3,1024,6,64]{1,3,2,0:T(8,128)(2,1)} %bitcast.268, f32[3,6,256,1024]{3,2,1,0:T(8,128)} %get-tuple-element.103, f32[3,6,256]{2,1,0:T(8,128)} %fusion, f32[3,6,256]{2,1,0:T(8,128)} %get-tuple-element.102), kind=kOutput, calls=%fused_computation.43 | convolution fusion | flops 623149056 | bytes 21860352 | tf_op jit(solution)/shard_map/ihpk,ikhd->iphd/dot_general | solution.py:248
  225.5 6.9 fusion.32
  251.0 3.8 multiply_reduce_fusion.4
  257.5 6.4 all-reduce.8
  273.3 8.0 %fusion.115 = f32[3456,384]{1,0:T(8,128)} fusion(bf16[768,3456]{1,0:T(8,128)(2,1)} %bitcast.294, bf16[768,384]{1,0:T(8,128)(2,1)S(1)} %get-tuple-element.78), kind=kOutput, calls=%fused_computation.229 | convolution fusion | flops 2038431744 | bytes 11206656 | tf_op jit(solution)/shard_map/dot_general | solution.py:334
  282.7 3.2 collective-permute-start.4
  297.4 11.6 %dot_general.89 = bf16[3,256,9,384]{3,2,1,0:T(8,128)(2,1)} reshape(bf16[3,8,32,3456]{3,2,1,0:T(8,128)(2,1)} %slice_dynamic-update-slice_fusion.6) | data formatting | bytes 10616832 | tf_op jit(solution)/shard_map/dot_general | solution.py:124
  309.0 9.5 %multiply_reduce_fusion.6 = (f32[384]{0:T(512)}, f32[3,384]{1,0:T(4,128)S(1)}, f32[3,384]{1,0:T(4,128)}, f32[384]{0:T(512)}, f32[3,384]{1,0:T(4,128)}, /*index=5*/f32[3,384]{1,0:T(4,128)S(1)}, f32[3,256,384]{2,1,0:T(8,128)}) fusion(f32[3,256,384]{2,1,0:T(8,128)} %bitcast.252, f32[3,384]{1,0:T(4,128)} %copy-done.38, f32[3,384]{1,0:T(4,128)} %copy-done.34, ...), kind=kOutput, calls=%fused_computation.104 | convolution fusion | flops 2045799168 | bytes 10364928 | tf_op jit(solution)/shard_map/dot_general | solution.py:124
  327.4 7.7 %all-reduce.7 = (f32[3,32]{1,0:T(4,128)}, f32[3,32]{1,0:T(4,128)S(1)}) all-reduce(f32[3,32]{1,0:T(4,128)S(1)} %reduce_sum.328, f32[3,32]{1,0:T(4,128)S(1)} %reduce_sum.331), channel_id=1, replica_groups=mesh['img'=8,'row'=4] {'row'}, use_global_device_ids=true, to_apply=%region_27.28 | all-reduce | flops 192 | bytes 1536 | tf_op jit(solution)/shard_map/psum | solution.py:73
  346.2 4.0 convert_reduce_fusion.2
  350.2 8.0 %fusion.114 = f32[3456,384]{1,0:T(8,128)} fusion(bf16[768,3456]{1,0:T(8,128)(2,1)} %bitcast.292, bf16[768,384]{1,0:T(8,128)(2,1)S(1)} %get-tuple-element.73), kind=kOutput, calls=%fused_computation.228 | convolution fusion | flops 2038431744 | bytes 11206656 | tf_op jit(solution)/shard_map/dot_general | solution.py:351
  371.2 3.3 collective-permute-start.6
  384.3 11.7 %dot_general.91 = bf16[3,256,9,384]{3,2,1,0:T(8,128)(2,1)} reshape(bf16[3,8,32,3456]{3,2,1,0:T(8,128)(2,1)} %slice_dynamic-update-slice_fusion) | data formatting | bytes 10616832 | tf_op jit(solution)/shard_map/dot_general | solution.py:124
  396.1 9.1 %fusion.77 = (f32[384]{0:T(512)S(1)}, f32[3,384]{1,0:T(4,128)S(1)}, f32[3,384]{1,0:T(4,128)S(1)}, f32[384]{0:T(512)S(1)}, f32[3,256,384]{2,1,0:T(8,128)}) fusion(bf16[3,8,32,384]{3,2,1,0:T(8,128)(2,1)S(1)} %copy-done.2, f32[3,384]{1,0:T(4,128)S(1)} %copy-done.27, f32[3,384]{1,0:T(4,128)S(1)} %copy-done.25, f32[384]{0:T(512)S(1)} %copy-done.45, ...), kind=kOutput, calls=%fused_computation.98 | convolution fusion | flops 2041672704 | bytes 10934784 | tf_op jit(solution)/shard_map/dot_general | solution.py:124
  405.6 9.3 %all-reduce.6 = (f32[3,32]{1,0:T(4,128)S(1)}, f32[3,32]{1,0:T(4,128)S(1)}) all-reduce(f32[3,32]{1,0:T(4,128)S(1)} %reduce_sum.337, f32[3,32]{1,0:T(4,128)S(1)} %reduce_sum.334), channel_id=1, replica_groups=mesh['img'=8,'row'=4] {'row'}, use_global_device_ids=true, to_apply=%region_36.37 | all-reduce | flops 192 | bytes 1536 | tf_op jit(solution)/shard_map/psum | solution.py:73
  415.4 43.5 %all-reduce.4 = (f32[384]{0:T(512)S(1)}, f32[384]{0:T(512)S(1)}, f32[384]{0:T(512)S(1)}, f32[768]{0:T(1024)S(1)}, f32[384]{0:T(512)S(1)}, /*index=5*/f32[384]{0:...) all-reduce(f32[384]{0:T(512)S(1)} %get-tuple-element.23, ...), channel_id=1, replica_groups=mesh['img'=8,'row'=4] {'img','row'}, use_global_device_ids=true, to_apply=%region_38.39 | all-reduce | flops 4992 | bytes 39936 | tf_op jit(solution)/shard_map/psum | solution.py:374
  465.4 4.4 fusion.60
  469.9 197.7 %all-reduce.14.cloned.1.call-done = (f32[3456,384]{1,0:T(8,128)}, f32[768,768]{1,0:T(8,128)}, f32[1000,768]{1,0:T(8,128)}, f32[3456,384]{1,0:T(8,128)}, f32[384,1152]{1,0:T(8,128)}, /*index=5*/f32[384,384]{1,0:T(8,128)}) async-done(((f32[3456,384]{1,0:T(8,128)}, f32[768,768]{1,0:T(8,128)}, f32[1000,768]{1,0:T(8,128)}, f32[3456,384]{1,0:T(8,128)}, f32[384,1152]{1,0:T(8,128)}, ...) | async-done | bytes 18407440 | tf_op jit(solution)/shard_map/psum | solution.py:374
  (382 shorter events, 193.3 us)
Async XLA Ops:
  7.2 53.1 %copy-start = (bf16[3456,384]{1,0:T(8,128)(2,1)S(1)}, bf16[3456,384]{1,0:T(8,128)(2,1)}, u32[]{:S(2)}) copy-start(bf16[3456,384]{1,0:T(8,128)(2,1)} %param.35) | copy-start | bytes 7962628
  7.2 97.6 %all-gather.5.cloned.1.call-start = ((), (), s32[]{:S(2)}) async-start(), calls=%async_computation.3 | async-start | bytes 2949120 | tf_op jit(solution)/shard_map/all_gather | solution.py:232
  8.1 20.6 %copy-start.49 = (f32[384]{0:T(512)}, f32[384]{0:T(512)S(1)}, u32[]{:S(2)}) copy-start(f32[384]{0:T(512)S(1)} %convert_element_type.148) | copy-start | bytes 4612
  8.8 19.9 %copy-start.44 = (f32[384]{0:T(512)}, f32[384]{0:T(512)S(1)}, u32[]{:S(2)}) copy-start(f32[384]{0:T(512)S(1)} %convert_element_type.147) | copy-start | bytes 4612
  20.9 6.8 collective-permute-start.1
  22.2 5.5 collective-permute-start
  27.5 30.7 %copy-start.38 = (f32[3,384]{1,0:T(4,128)}, f32[3,384]{1,0:T(4,128)S(1)}, u32[]{:S(2)}) copy-start(f32[3,384]{1,0:T(4,128)S(1)} %get-tuple-element.90) | copy-start | bytes 13828
  27.5 30.7 %copy-start.39 = (f32[3,384]{1,0:T(4,128)}, f32[3,384]{1,0:T(4,128)S(1)}, u32[]{:S(2)}) copy-start(f32[3,384]{1,0:T(4,128)S(1)} %get-tuple-element.91) | copy-start | bytes 13828
  27.6 242.7 %copy-start.47 = (f32[384]{0:T(512)}, f32[384]{0:T(512)S(1)}, u32[]{:S(2)}) copy-start(f32[384]{0:T(512)S(1)} %convert_element_type.159) | copy-start | bytes 4612
  27.7 30.6 %copy-start.50 = (f32[384]{0:T(512)}, f32[384]{0:T(512)S(1)}, u32[]{:S(2)}) copy-start(f32[384]{0:T(512)S(1)} %convert_element_type.152) | copy-start | bytes 4612
  27.7 30.6 %copy-start.52 = (f32[384]{0:T(512)}, f32[384]{0:T(512)S(1)}, u32[]{:S(2)}) copy-start(f32[384]{0:T(512)S(1)} %convert_element_type.151) | copy-start | bytes 4612
  52.0 4.5 collective-permute-start.3
  53.3 3.9 collective-permute-start.2
  78.7 54.1 %all-gather.3.cloned.1.call-start = ((), (), s32[]{:S(2)}) async-start(), calls=%async_computation.2 | async-start | bytes 2949120 | tf_op jit(solution)/shard_map/all_gather | solution.py:233
  79.4 155.9 %reduce-scatter.3.cloned.1.call-start = ((), (), s32[]{:S(2)}) async-start(), calls=%async_computation.4 | async-start | bytes 2949120 | tf_op jit(solution)/shard_map/reduce_scatter | solution.py:291
  171.2 69.1 %reduce-scatter.5.cloned.1.call-start = ((), (), s32[]{:S(2)}) async-start(), calls=%async_computation.5 | async-start | bytes 2949120 | tf_op jit(solution)/shard_map/reduce_scatter | solution.py:294
  183.0 484.5 %all-reduce.14.cloned.1.call-start = ((), (), s32[]{:S(2)}) async-start(), calls=%async_computation.6 | async-start | bytes 36814848 | tf_op jit(solution)/shard_map/psum | solution.py:374
  281.4 6.8 collective-permute-start.5
  282.7 5.5 collective-permute-start.4
  369.9 4.7 collective-permute-start.7
  371.2 3.9 collective-permute-start.6
  396.0 19.3 %copy-start.58 = (f32[384]{0:T(512)S(1)}, f32[384]{0:T(512)}, u32[]{:S(2)}) copy-start(f32[384]{0:T(512)} %get-tuple-element.36) | copy-start | bytes 4612
  396.0 19.3 %copy-start.59 = (f32[384]{0:T(512)S(1)}, f32[384]{0:T(512)}, u32[]{:S(2)}) copy-start(f32[384]{0:T(512)} %get-tuple-element.77) | copy-start | bytes 4612
  396.0 19.3 %copy-start.61 = (f32[384]{0:T(512)S(1)}, f32[384]{0:T(512)}, u32[]{:S(2)}) copy-start(f32[384]{0:T(512)} %get-tuple-element.72) | copy-start | bytes 4612
  396.0 19.3 %copy-start.62 = (f32[384]{0:T(512)S(1)}, f32[384]{0:T(512)}, u32[]{:S(2)}) copy-start(f32[384]{0:T(512)} %convert_reduce_fusion.3) | copy-start | bytes 4612
  396.0 19.3 %copy-start.69 = (f32[384]{0:T(512)S(1)}, f32[384]{0:T(512)}, u32[]{:S(2)}) copy-start(f32[384]{0:T(512)} %get-tuple-element.21) | copy-start | bytes 4612
  396.0 19.3 %copy-start.70 = (f32[384]{0:T(512)S(1)}, f32[384]{0:T(512)}, u32[]{:S(2)}) copy-start(f32[384]{0:T(512)} %get-tuple-element.32) | copy-start | bytes 4612
  396.0 69.4 %copy-start.29 = (f32[3,384]{1,0:T(4,128)S(1)}, f32[3,384]{1,0:T(4,128)}, u32[]{:S(2)}) copy-start(f32[3,384]{1,0:T(4,128)} %copy-done.28) | copy-start | bytes 13828
  396.1 69.4 %copy-start.31 = (f32[3,384]{1,0:T(4,128)S(1)}, f32[3,384]{1,0:T(4,128)}, u32[]{:S(2)}) copy-start(f32[3,384]{1,0:T(4,128)} %copy-done.30) | copy-start | bytes 13828
  396.1 69.4 %copy-start.36 = (f32[3,384]{1,0:T(4,128)S(1)}, f32[3,384]{1,0:T(4,128)}, u32[]{:S(2)}) copy-start(f32[3,384]{1,0:T(4,128)} %mul.485) | copy-start | bytes 13828
  396.1 69.4 %copy-start.37 = (f32[3,384]{1,0:T(4,128)S(1)}, f32[3,384]{1,0:T(4,128)}, u32[]{:S(2)}) copy-start(f32[3,384]{1,0:T(4,128)} %sub.205) | copy-start | bytes 13828
  396.1 69.3 %copy-start.48 = (f32[384]{0:T(512)S(1)}, f32[384]{0:T(512)}, u32[]{:S(2)}) copy-start(f32[384]{0:T(512)} %copy-done.47) | copy-start | bytes 4612
  (62 other events, 394.9 us)
Sparse Core Ops, SparseCore 0:
  78.8 26.0 all-gather.4
  107.0 24.0 all-gather.2
  171.4 33.2 reduce-scatter.2
  207.3 33.0 reduce-scatter.4
  361.5 306.0 all-reduce.13
where the time goes:
time: 696 us; the launch traced here: 687 us
  waiting for transfers between devices  217 us (31%)
  local copies, waits for them, and re-layouts  158 us (23%)
  matrix products  119 us (17%)
  blocking collectives  88.6 us (13%)
  other arithmetic  69.3 us (10%)
  starting transfers between devices  18.4 us (3%)
  between operations  15.7 us (2%)
    psum x1, waiting for transfers between devices, shards(): lax.psum((first_gain_grad, first_shift_grad, first_kernel_grad, first_off...  198 us
    psum x1, blocking collectives, shards(): lax.psum((first_gain_grad, first_shift_grad, first_kernel_grad, first_off...  43.5 us
    unnamed x194, local copies, waits for them, and re-layouts  33.7 us
    psum x3, blocking collectives, group_back(): first_sum, second_sum = lax.psum((first_sum, second_sum), 'row')  23.4 us
    dot_general x2, local copies, waits for them, and re-layouts, transpose_product(): lax.dot_general(stacked, kernel_taps, (((1, 2), (0, 2)), ((), ())), prefe...  23.3 us
    psum x3, blocking collectives, group_stats(): first_sum, second_sum = lax.psum((first_sum, second_sum), 'row')  21.6 us
    dynamic_slice x17, local copies, waits for them, and re-layouts, shards(): lax.dynamic_slice_in_dim(item_value, stripe_index * (item_value.shape[0]...  18.8 us
    dot_general x2, matrix products, transpose_product(): lax.dot_general(stacked, kernel_taps, (((1, 2), (0, 2)), ((), ())), prefe...  18.7 us
  transfers between devices with their start and end apart: 13, of which 5 were waited for; matrix products, arithmetic and copies ran while one was open for 23% of the time, Pallas kernels for 0%

commit v1 on v0

v1 whole, which is shorter than its diff:
```python
import math

import jax
import jax.numpy as jnp
from jax import lax
from jax.experimental import pallas as pl
from jax.experimental.pallas import tpu as pltpu
from jax.sharding import PartitionSpec as P

GROUPS = 32
HEAD = 64
EMB = 768
MESH = pl.DeviceIdType.MESH

norm_eps = 1e-05
sigma_least = 0.002
sigma_most = 80.0
sigma_power = 7.0
highest = lax.Precision.HIGHEST
float_type = jnp.float32
low_type = jnp.bfloat16
contract_rows = (((0,), (0,)), ((), ()))
contract_cols = (((1,), (1,)), ((), ()))


def noise_features(level_count, level_index):
    position = (level_index.astype(jnp.float32) + 1.0) / (level_count.astype(jnp.float32) - 1.0)
    low_root = sigma_least ** (1.0 / sigma_power)
    high_root = sigma_most ** (1.0 / sigma_power)
    noise_level = (low_root + position * (high_root - low_root)) ** sigma_power
    noise_time = 250.0 * jnp.log(noise_level)
    half_width = EMB // 2
    frequency = jnp.exp(-math.log(10000.0) * jnp.arange(half_width, dtype=jnp.float32) / half_width)
    angles = noise_time[:, None] * frequency[None, :]
    return jnp.concatenate([jnp.cos(angles), jnp.sin(angles)], axis=-1)


def silu_slope(values):
    sigmoid_part = jax.nn.sigmoid(values)
    return sigmoid_part * (1.0 + values * (1.0 - sigmoid_part))


def normalize(values, centre, scaled):
    return (values - centre) * scaled


def group_fold(v):
    return v.reshape(v.shape[:-1] + (GROUPS, v.shape[-1] // GROUPS))


def group_back(upstream, normed, scaled):
    image_count, pixels, channels = upstream.shape
    first_sum = jnp.sum(group_fold(jnp.sum(upstream, axis=1)), axis=-1)
    second_sum = jnp.sum(group_fold(jnp.sum(upstream * normed, axis=1)), axis=-1)
    first_sum, second_sum = lax.psum((first_sum, second_sum), "row")
    entries = pixels * lax.axis_size("row") * (channels // GROUPS)
    per = channels // GROUPS
    first_sum = jnp.repeat(first_sum / entries, per, axis=-1)
    second_sum = jnp.repeat(second_sum / entries, per, axis=-1)
    return scaled * (upstream - first_sum[:, None, :] - normed * second_sum[:, None, :])


def padded_grads(activity):
    size, length = lax.axis_size("row"), activity.shape[1]
    up = [(i, i + 1) for i in range(size - 1)]
    down = [(j, i) for i, j in up]
    last = lax.slice_in_dim(activity, length - 1, length, axis=1)
    initial = lax.slice_in_dim(activity, 0, 1, axis=1)
    before = lax.ppermute(last, "row", up)
    after = lax.ppermute(initial, "row", down)
    framed = jnp.concatenate([before, activity, after], axis=1)
    return jnp.pad(framed, ((0, 0), (0, 0), (1, 1), (0, 0)))


def backward_patches(framed, stripe_rows, image_width):
    pieces = [
        framed[
            :, 2 - row_tap : 2 - row_tap + stripe_rows, 2 - col_tap : 2 - col_tap + image_width, :
        ]
        for row_tap in range(3)
        for col_tap in range(3)
    ]
    joined = jnp.concatenate(pieces, axis=-1)
    return joined.reshape(-1, joined.shape[-1])


def transpose_product(columns, kernel):
    channels = kernel.shape[1]
    stacked = columns.reshape(columns.shape[0], 9, channels)
    kernel_taps = kernel.reshape(9, kernel.shape[0] // 9, channels)
    return lax.dot_general(
        stacked, kernel_taps, (((1, 2), (0, 2)), ((), ())), preferred_element_type=float_type
    )


def peers():
    i = lax.axis_index("img")
    r = lax.axis_index("row")
    c = lax.rem(r, 2)
    near = r + 1 - 2 * c
    return (i, r, c, {1: (i, near), 2: (i, lax.rem(r + 2, 4)), 3: (i, 3 - r)})


def half_silu(v):
    h = 0.5 * v
    return h * jnp.tanh(h) + h


def col_iota(n, width, channels):
    return lax.rem(lax.broadcasted_iota(jnp.int32, (n, channels), 0), width)


def fill_row(buf, start, act, channels, width):
    col = lax.broadcasted_iota(jnp.int32, (width, channels), 0)
    left = jnp.where(col == 0, 0.0, pltpu.roll(act, 1, 0))
    right = jnp.where(col == width - 1, 0.0, pltpu.roll(act, width - 1, 0))
    rows = pl.ds(start, width)
    buf[rows, 0:channels] = left.astype(low_type)
    buf[rows, channels : 2 * channels] = act.astype(low_type)
    buf[rows, 2 * channels : 3 * channels] = right.astype(low_type)


def pack_stats(first, second):
    channels = first.shape[1]
    row = lax.broadcasted_iota(jnp.int32, (8, channels), 0)

    def terms(v):
        a = v.astype(low_type).astype(float_type)
        b = (v - a).astype(low_type).astype(float_type)
        c = v - a - b
        return jnp.where(row == 0, a, jnp.where(row == 1, b, jnp.where(row == 2, c, 0.0)))

    return jnp.concatenate([terms(first), terms(second)], axis=0).astype(low_type)


def block_ones(channels, per):
    a = lax.broadcasted_iota(jnp.int32, (channels, channels), 0)
    b = lax.broadcasted_iota(jnp.int32, (channels, channels), 1)
    a = lax.shift_right_logical(a * 43691, 19)
    b = lax.shift_right_logical(b * 43691, 19)
    return jnp.where(a == b, 1.0, 0.0).astype(low_type)


def combine_stats(parts, ones, entries):
    total = jnp.dot(jnp.concatenate(parts, axis=0), ones, preferred_element_type=float_type)
    first = total[0:8] + total[16:24] + total[32:40] + total[48:56]
    second = total[8:16] + total[24:32] + total[40:48] + total[56:64]
    first = jnp.sum(first, axis=0, keepdims=True) * (1.0 / entries)
    second = jnp.sum(second, axis=0, keepdims=True) * (1.0 / entries)
    return first, second


def forward_kernel(
    x_ref, vec_ref, mod_ref, w1_any, w2_any,
    hid_ref, mid_ref, att_ref, act1_ref, act2_ref, st_ref,
    w1, w2, ones, abuf, m1, m3, got, wsem, ssem, rsem,
):
    images, pixels, channels = x_ref.shape
    width = 32
    edge = pixels - width
    entries = 4.0 * pixels * (channels // GROUPS)
    i, r, c, who = peers()
    load1 = pltpu.make_async_copy(w1_any, w1, wsem.at[0])
    load2 = pltpu.make_async_copy(w2_any, w2, wsem.at[1])
    load1.start()
    load2.start()
    barrier = pltpu.get_barrier_semaphore()
    for k in (1, 2, 3):
        pl.semaphore_signal(barrier, inc=1, device_id=who[k], device_id_type=MESH)
    ones[...] = block_ones(channels, channels // GROUPS)
    inner = pl.multiple_of(edge * (1 - c), width)
    outer = pl.multiple_of(edge * c, width)
    inner_live = None
    outer_live = jnp.logical_and(r > 0, r < 3)
    stat = pl.ds(0, 16)
    halo = pl.ds(16, width)

    def copies(p, b):
        full = p < 2
        rows = pl.ds(0, 48) if full else stat
        return [
            pltpu.make_async_remote_copy(
                src.at[p, b, rs], got.at[p, b, k - 1, rs], ssem.at[p, b, k - 1],
                rsem.at[p, b, k - 1], device_id=who[k], device_id_type=MESH,
            )
            for k, src, rs in ((1, m1, rows), (2, m1, stat), (3, m3, rows))
        ]

    def send(p, b, first, second, edges):
        packed = pack_stats(first, second)
        m1[p, b, 0:16] = packed
        m3[p, b, 0:16] = packed
        if edges is not None:
            m1[p, b, 16:48] = edges(inner)
            m3[p, b, 16:48] = edges(outer)
        for cp in copies(p, b):
            cp.start()

    def receive(p, b):
        for cp in copies(p, b):
            cp.wait_recv()
        parts = [m1[p, b, 0:16]] + [got[p, b, k, 0:16] for k in range(3)]
        first, second = combine_stats(parts, ones[...], entries)
        return first, lax.rsqrt(second - first * first + norm_eps)

    def expand(p, b, affine, own, keep):
        for row in range(pixels // width):
            a = half_silu(affine(own(row)))
            keep[b, pl.ds(row * width, width)] = a.astype(low_type)
            fill_row(abuf, (row + 1) * width, a, channels, width)
        a = half_silu(affine(got[p, b, 0, 16:48].astype(float_type)))
        fill_row(abuf, pl.multiple_of((pixels + width) * (1 - c), width), a, channels, width)
        a = half_silu(affine(got[p, b, 2, 16:48].astype(float_type)))
        a = jnp.where(outer_live, a, 0.0)
        fill_row(abuf, pl.multiple_of((pixels + width) * c, width), a, channels, width)

    def convolve(w):
        depth = 3 * channels
        return sum(
            jnp.dot(
                abuf[width * dy : width * dy + pixels, :],
                w[depth * dy : depth * (dy + 1), :],
                preferred_element_type=float_type,
            )
            for dy in range(3)
        )

    def vec(n):
        return vec_ref[n : n + 1, :]

    pl.semaphore_wait(barrier, 3)

    def step0(b, _):
        v = x_ref[b].astype(float_type)
        send(
            0, b, jnp.sum(v, axis=0, keepdims=True), jnp.sum(v * v, axis=0, keepdims=True),
            lambda at: x_ref[b, pl.ds(at, width)],
        )
        return 0

    lax.fori_loop(0, images, step0, 0)
    load1.wait()

    def step1(b, _):
        centre, scaled = receive(0, b)
        st_ref[b, 0:1] = centre
        st_ref[b, 1:2] = scaled
        slope = scaled * vec(0)
        shift = vec(1)
        expand(
            0, b, lambda v: (v - centre) * slope + shift,
            lambda row: x_ref[b, pl.ds(row * width, width)].astype(float_type), act1_ref,
        )
        hidden = convolve(w1) + vec(2)
        hid_ref[b] = hidden
        send(
            1, b, jnp.sum(hidden, axis=0, keepdims=True),
            jnp.sum(hidden * hidden, axis=0, keepdims=True),
            lambda at: hid_ref[b, pl.ds(at, width)].astype(low_type),
        )
        return 0

    lax.fori_loop(0, images, step1, 0)
    load2.wait()

    def step2(b, _):
        centre, scaled = receive(1, b)
        st_ref[b, 2:3] = centre
        st_ref[b, 3:4] = scaled
        grow = 1.0 + mod_ref[b, 0:1]
        slope = scaled * vec(3) * grow
        shift = vec(4) * grow + mod_ref[b, 1:2]
        expand(
            1, b, lambda v: (v - centre) * slope + shift,
            lambda row: hid_ref[b, pl.ds(row * width, width)], act2_ref,
        )
        middle = (convolve(w2) + vec(5) + x_ref[b].astype(float_type)) * math.sqrt(0.5)
        mid_ref[b] = middle
        send(
            2, b, jnp.sum(middle, axis=0, keepdims=True),
            jnp.sum(middle * middle, axis=0, keepdims=True), None,
        )
        return 0

    lax.fori_loop(0, images, step2, 0)

    def step3(b, _):
        centre, scaled = receive(2, b)
        st_ref[b, 4:5] = centre
        st_ref[b, 5:6] = scaled
        slope = scaled * vec(6)
        att_ref[b] = ((mid_ref[b] - centre) * slope + vec(7)).astype(low_type)
        for p in range(3):
            for cp in copies(p, b):
                cp.wait_send()
        return 0

    lax.fori_loop(0, images, step3, 0)


def forward_call(x, vectors, modulate, first_kernel, second_kernel):
    images, pixels, channels = x.shape
    depth = 9 * channels
    vm = pl.BlockSpec(memory_space=pltpu.VMEM)
    hbm = pl.BlockSpec(memory_space=pl.ANY)
    wide = jax.ShapeDtypeStruct(x.shape, float_type)
    low = jax.ShapeDtypeStruct(x.shape, low_type)
    return pl.pallas_call(
        forward_kernel,
        out_shape=(wide, wide, low, low, low, jax.ShapeDtypeStruct((images, 8, channels), float_type)),
        in_specs=[vm, vm, vm, hbm, hbm],
        out_specs=(vm,) * 6,
        scratch_shapes=[
            pltpu.VMEM((depth, channels), low_type),
            pltpu.VMEM((depth, channels), low_type),
            pltpu.VMEM((channels, channels), low_type),
            pltpu.VMEM((pixels + 64, 3 * channels), low_type),
            pltpu.VMEM((3, images, 48, channels), low_type),
            pltpu.VMEM((3, images, 48, channels), low_type),
            pltpu.VMEM((3, images, 3, 48, channels), low_type),
            pltpu.SemaphoreType.DMA((2,)),
            pltpu.SemaphoreType.DMA((3, images, 3)),
            pltpu.SemaphoreType.DMA((3, images, 3)),
        ],
        compiler_params=pltpu.CompilerParams(
            collective_id=0, has_side_effects=True, vmem_limit_bytes=56 << 20
        ),
        name="forward",
    )(x, vectors, modulate, first_kernel, second_kernel)


def shards(
    images,
    level_count,
    level_index,
    labels,
    first_gain,
    first_shift,
    first_kernel,
    first_offset,
    embed_weight,
    embed_offset,
    class_table,
    second_gain,
    second_shift,
    second_kernel,
    second_offset,
    third_gain,
    third_shift,
    joint_weight,
    joint_offset,
    output_weight,
    output_offset,
    cotangent,
):
    image_count, stripe_rows, image_width, channels = images.shape
    layout = (image_count, stripe_rows, image_width, channels)
    pixels = stripe_rows * image_width
    head_count = channels // HEAD
    score_scale = HEAD ** (-0.5)
    gain_one = first_gain.astype(float_type)
    shift_one = first_shift.astype(float_type)
    gain_two = second_gain.astype(float_type)
    shift_two = second_shift.astype(float_type)
    gain_three = third_gain.astype(float_type)
    features = noise_features(level_count, level_index)
    class_count = class_table.shape[0]
    one_hot = (labels[:, None] == jnp.arange(class_count, dtype=jnp.int32)[None, :]).astype(
        low_type
    )
    embedded = features + jnp.dot(one_hot, class_table, preferred_element_type=float_type)
    embed_act = jax.nn.silu(embedded).astype(low_type)
    modulate = jnp.dot(
        embed_act, embed_weight, preferred_element_type=float_type
    ) + embed_offset.astype(float_type)
    scale_part = modulate[:, :channels]
    vectors = jnp.stack(
        [
            first_gain, first_shift, first_offset, second_gain, second_shift, second_offset,
            third_gain, third_shift,
        ]
    ).astype(float_type)
    x = images.reshape(image_count, pixels, channels)
    hidden, middle, attend, act_one, act_two, stats = forward_call(
        x, vectors, modulate.reshape(image_count, 2, channels), first_kernel, second_kernel
    )
    flattened = x.astype(float_type)
    scaled_one, scaled_two, scaled_three = (stats[:, n : n + 1] for n in (1, 3, 5))
    normed_one = normalize(flattened, stats[:, 0:1], scaled_one)
    normed_two = normalize(hidden, stats[:, 2:3], scaled_two)
    normed_three = normalize(middle, stats[:, 4:5], scaled_three)
    pre_one = normed_one * gain_one + shift_one
    shaped = normed_two * gain_two + shift_two
    pre_two = shaped * (1.0 + scale_part[:, None, :]) + modulate[:, None, channels:]
    attend_input = attend.reshape(image_count * pixels, channels)
    columns_one = backward_patches(padded_grads(act_one.reshape(layout)), stripe_rows, image_width)
    columns_two = backward_patches(padded_grads(act_two.reshape(layout)), stripe_rows, image_width)

    def forward_order(columns):
        return columns.reshape(-1, 9, channels)[:, ::-1].reshape(-1, 9 * channels)

    columns_one, columns_two = forward_order(columns_one), forward_order(columns_two)
    zero_part = jnp.zeros((channels,), low_type)
    joint_bias = jnp.concatenate(
        [joint_offset[:channels], zero_part, joint_offset[channels:]]
    ).astype(float_type)
    joint_rows = (
        jnp.dot(attend_input, joint_weight, preferred_element_type=float_type) + joint_bias
    ).astype(low_type)
    joint_rows = joint_rows.reshape(image_count, pixels, 3 * channels)
    query_local = joint_rows[:, :, :channels]
    key_local = joint_rows[:, :, channels : 2 * channels]
    value_local = joint_rows[:, :, 2 * channels :]
    key_rows, value_rows = (
        lax.all_gather(key_local, "row", axis=1, tiled=True),
        lax.all_gather(value_local, "row", axis=1, tiled=True),
    )
    query_heads = query_local.reshape(image_count, pixels, head_count, HEAD)
    key_heads = key_rows.reshape(image_count, -1, head_count, HEAD)
    value_heads = value_rows.reshape(image_count, -1, head_count, HEAD)
    scores = (
        jnp.einsum("iphd,ikhd->ihpk", query_heads, key_heads, preferred_element_type=float_type)
        * score_scale
    )
    row_peak = jnp.max(scores, axis=-1, keepdims=True)
    raised = jnp.exp(scores - row_peak)
    row_total = jnp.sum(raised, axis=-1, keepdims=True)
    weights = raised / row_total
    log_total = row_peak + jnp.log(row_total)
    weights_low = weights.astype(low_type)
    mixed_rows = jnp.einsum(
        "ihpk,ikhd->iphd", weights_low, value_heads, preferred_element_type=float_type
    )
    mixed_rows = mixed_rows.reshape(image_count * pixels, channels).astype(low_type)
    outcome = (
        middle.reshape(image_count * pixels, channels)
        + jnp.dot(mixed_rows, output_weight, preferred_element_type=float_type)
        + output_offset.astype(float_type)
    )
    result = outcome.astype(low_type).reshape(layout)
    cotangent_low = cotangent.reshape(image_count * pixels, channels)
    upstream = cotangent_low.astype(float_type)
    output_weight_grad = lax.dot_general(
        mixed_rows, cotangent_low, contract_rows, preferred_element_type=float_type
    )
    output_offset_grad = jnp.sum(upstream, axis=0)
    mixed_grad = lax.dot_general(
        cotangent_low, output_weight, contract_cols, preferred_element_type=float_type
    )
    mixed_grad = mixed_grad.astype(low_type).reshape(image_count, pixels, head_count, HEAD)
    scores = (
        jnp.einsum("iphd,ikhd->ihpk", query_heads, key_heads, preferred_element_type=float_type)
        * score_scale
    )
    weights = jnp.exp(scores - log_total)
    weights_low = weights.astype(low_type)
    value_part = jnp.einsum(
        "ihpk,iphd->ikhd", weights_low, mixed_grad, preferred_element_type=float_type
    )
    weight_grad = jnp.einsum(
        "iphd,ikhd->ihpk", mixed_grad, value_heads, preferred_element_type=float_type
    )
    row_inner = jnp.sum(weights * weight_grad, axis=-1, keepdims=True)
    score_grad = (weights * (weight_grad - row_inner)).astype(low_type)
    query_grad = (
        jnp.einsum("ihpk,ikhd->iphd", score_grad, key_heads, preferred_element_type=float_type)
        * score_scale
    )
    key_part = (
        jnp.einsum("ihpk,iphd->ikhd", score_grad, query_heads, preferred_element_type=float_type)
        * score_scale
    )
    key_grad, value_grad = (
        lax.psum_scatter(
            key_part.astype(jnp.bfloat16), "row", scatter_dimension=1, tiled=True
        ).astype(jnp.float32),
        lax.psum_scatter(
            value_part.astype(jnp.bfloat16), "row", scatter_dimension=1, tiled=True
        ).astype(jnp.float32),
    )
    joint_grad = jnp.concatenate(
        [
            query_grad.reshape(image_count * pixels, channels),
            key_grad.reshape(image_count * pixels, channels),
            value_grad.reshape(image_count * pixels, channels),
        ],
        axis=-1,
    ).astype(low_type)
    joint_grad_wide = joint_grad.astype(float_type)
    joint_offset_grad = jnp.concatenate(
        [
            jnp.sum(joint_grad_wide[:, :channels], axis=0),
            jnp.sum(joint_grad_wide[:, 2 * channels :], axis=0),
        ]
    )
    joint_weight_grad = lax.dot_general(
        attend_input, joint_grad, contract_rows, preferred_element_type=float_type
    )
    attend_grad = lax.dot_general(
        joint_grad, joint_weight, contract_cols, preferred_element_type=float_type
    )
    attend_grad = attend_grad.reshape(image_count, pixels, channels)
    third_gain_grad = jnp.sum(attend_grad * normed_three, axis=(0, 1))
    third_shift_grad = jnp.sum(attend_grad, axis=(0, 1))
    middle_grad = upstream.reshape(image_count, pixels, channels) + group_back(
        attend_grad * gain_three, normed_three, scaled_three
    )
    skip_grad = middle_grad * math.sqrt(0.5)
    branch_grad = skip_grad.reshape(image_count * pixels, channels).astype(low_type)
    second_offset_grad = jnp.sum(branch_grad.astype(float_type), axis=0)
    second_kernel_grad = lax.dot_general(
        columns_two, branch_grad, contract_rows, preferred_element_type=float_type
    )
    framed_two = padded_grads(branch_grad.reshape(layout))
    act_two_grad = transpose_product(
        backward_patches(framed_two, stripe_rows, image_width), second_kernel
    )
    pre_two_grad = act_two_grad.reshape(image_count, pixels, channels) * silu_slope(pre_two)
    scale_grad = jnp.sum(pre_two_grad * shaped, axis=1)
    shift_grad = jnp.sum(pre_two_grad, axis=1)
    modulate_grad = jnp.concatenate([scale_grad, shift_grad], axis=-1)
    shaped_grad = pre_two_grad * (1.0 + scale_part[:, None, :])
    second_gain_grad = jnp.sum(shaped_grad * normed_two, axis=(0, 1))
    second_shift_grad = jnp.sum(shaped_grad, axis=(0, 1))
    hidden_grad = group_back(shaped_grad * gain_two, normed_two, scaled_two)
    hidden_grad = hidden_grad.reshape(image_count * pixels, channels).astype(low_type)
    first_offset_grad = jnp.sum(hidden_grad.astype(float_type), axis=0)
    first_kernel_grad = lax.dot_general(
        columns_one, hidden_grad, contract_rows, preferred_element_type=float_type
    )
    framed_one = padded_grads(hidden_grad.reshape(layout))
    act_one_grad = transpose_product(
        backward_patches(framed_one, stripe_rows, image_width), first_kernel
    )
    pre_one_grad = act_one_grad.reshape(image_count, pixels, channels) * silu_slope(pre_one)
    first_gain_grad = jnp.sum(pre_one_grad * normed_one, axis=(0, 1))
    first_shift_grad = jnp.sum(pre_one_grad, axis=(0, 1))
    images_gradient = skip_grad + group_back(pre_one_grad * gain_one, normed_one, scaled_one)
    images_gradient = images_gradient.reshape(layout)
    modulate_grad = lax.psum(modulate_grad, "row")
    every_grad, every_embedded, every_label = lax.all_gather(
        (modulate_grad, embedded, labels), "img", axis=0, tiled=True
    )
    stripe_index = lax.axis_index("row")
    stripe_count = lax.axis_size("row")

    def own_rows(v, axis):
        size = v.shape[axis] // stripe_count
        return lax.dynamic_slice_in_dim(v, stripe_index * size, size, axis)

    every_act = jax.nn.silu(every_embedded).astype(low_type).astype(float_type)
    embed_weight_grad = lax.dot_general(
        own_rows(every_act, 1), every_grad, contract_rows, precision=highest
    )
    embed_offset_grad = own_rows(jnp.sum(every_grad, axis=0), 0)
    active_grad = lax.dot_general(
        every_grad, embed_weight.astype(float_type), contract_cols, precision=highest
    )
    embedded_grad = active_grad * silu_slope(every_embedded)
    own_classes = stripe_index * (class_count // stripe_count) + jnp.arange(
        class_count // stripe_count, dtype=jnp.int32
    )
    own_hot = (every_label[:, None] == own_classes[None, :]).astype(float_type)
    class_table_grad = lax.dot_general(own_hot, embedded_grad, contract_rows, precision=highest)

    def scattered(v):
        v = lax.psum_scatter(v.astype(low_type), "row", scatter_dimension=0, tiled=True)
        return lax.psum(v.astype(low_type), "img").astype(float_type)

    first_kernel_grad, second_kernel_grad, joint_weight_grad, output_weight_grad = (
        scattered(v)
        for v in (first_kernel_grad, second_kernel_grad, joint_weight_grad, output_weight_grad)
    )
    small = (
        first_gain_grad, first_shift_grad, first_offset_grad, second_gain_grad, second_shift_grad,
        second_offset_grad, third_gain_grad, third_shift_grad, joint_offset_grad,
        output_offset_grad,
    )
    summed = lax.psum(jnp.concatenate(small), ("img", "row"))
    pieces, at = [], 0
    for v in small:
        pieces.append(own_rows(summed[at : at + v.shape[0]], 0))
        at += v.shape[0]
    (
        first_gain_grad, first_shift_grad, first_offset_grad, second_gain_grad, second_shift_grad,
        second_offset_grad, third_gain_grad, third_shift_grad, joint_offset_grad,
        output_offset_grad,
    ) = pieces
    return (
        result, images_gradient, first_gain_grad, first_shift_grad, first_kernel_grad,
        first_offset_grad, embed_weight_grad, embed_offset_grad, class_table_grad,
        second_gain_grad, second_shift_grad, second_kernel_grad, second_offset_grad,
        third_gain_grad, third_shift_grad, joint_weight_grad, joint_offset_grad,
        output_weight_grad, output_offset_grad,
    )


def solution(mesh):
    in_specs = (
        (P("img", "row", None, None),) + (P("img"),) * 3 + (P(),) * 17
        + (P("img", "row", None, None),)
    )
    row, rows = P("row"), P("row", None)
    out_specs = (
        P("img", "row", None, None), P("img", "row", None, None), row, row, rows, row, rows, row,
        rows, row, row, rows, row, row, row, rows, row, rows, row,
    )
    return jax.shard_map(shards, mesh=mesh, in_specs=in_specs, out_specs=out_specs, check_vma=False)
```

time: 696 us -> 561 us (0.81)
  waiting for transfers between devices: 217 us -> 7.77 us
  blocking collectives: 88.6 us -> 138 us
  local copies, waits for them, and re-layouts: 158 us -> 192 us
  Pallas kernels: 0 us -> 22 us
  matrix products: 119 us -> 102 us
  other arithmetic: 69.3 us -> 56.2 us
    psum x1, waiting for transfers between devices: 198 us -> 5.94 us  [scattered(): return lax.psum(v.astype(low_type), 'img').astype(float_type)]
    rev x0 -> x4, local copies, waits for them, and re-layouts: none -> 72.5 us  [forward_order(): return columns.reshape(-1, 9, channels)[:, ::-1].reshape(-1, 9 * channels)]
    all_gather x0 -> x2, blocking collectives: none -> 62 us  [shards(): lax.all_gather((modulate_grad, embedded, labels), 'img', axis=0, tiled=True)]
    psum x4 -> x1, blocking collectives: 65.1 us -> 38.7 us  [shards(): summed = lax.psum(jnp.concatenate(small), ('img', 'row'))]
    another operation x1 -> x11, local copies, waits for them, and re-layouts: 2.58 us -> 28.8 us  [the longest x2 23.2 us: forward_order(): return columns.reshape(-1, 9, channels)[:, ::-1].reshape(-1, 9 * channels)]
    pallas_call x0 -> x1, Pallas kernels: none -> 22 us  [forward_call(): pl.pallas_call(forward_kernel, out_shape=(wide, wide, low, low, low, jax....]
    all_gather x1, waiting for transfers between devices: 15.1 us -> 0.01 us  [shards(): lax.all_gather(key_local, 'row', axis=1, tiled=True)]
    dynamic_slice x17 -> x11, local copies, waits for them, and re-layouts: 18.8 us -> 6.51 us  [own_rows(): return lax.dynamic_slice_in_dim(v, stripe_index * size, size, axis)]
  transfers between devices with their start and end apart: 13 -> 17, of which waited for: 5 -> 2; matrix products, arithmetic and copies ran while one was open for 23% -> 58% of each run, Pallas kernels for 0% -> 0%
where the time goes in v1:
time: 561 us; the launch traced here: 552 us
  local copies, waits for them, and re-layouts  192 us (34%)
  blocking collectives  138 us (25%)
  matrix products  102 us (18%)
  other arithmetic  56.2 us (10%)
  Pallas kernels  22 us (4%)
  starting transfers between devices  19.1 us (3%)
  between operations  15.9 us (3%)
  waiting for transfers between devices  7.77 us (1%)
    rev x4, local copies, waits for them, and re-layouts, forward_order(): return columns.reshape(-1, 9, channels)[:, ::-1].reshape(-1, 9 * channels)  72.5 us
    all_gather x2, blocking collectives, shards(): lax.all_gather((modulate_grad, embedded, labels), 'img', axis=0, tiled=True)  62 us
    psum x1, blocking collectives, shards(): summed = lax.psum(jnp.concatenate(small), ('img', 'row'))  38.7 us
    unnamed x172, local copies, waits for them, and re-layouts  33.2 us
    psum x3, blocking collectives, group_back(): first_sum, second_sum = lax.psum((first_sum, second_sum), 'row')  24.6 us
    dot_general x2, local copies, waits for them, and re-layouts, transpose_product(): lax.dot_general(stacked, kernel_taps, (((1, 2), (0, 2)), ((), ())), prefe...  23.3 us
    another operation x2, local copies, waits for them, and re-layouts, forward_order(): return columns.reshape(-1, 9, channels)[:, ::-1].reshape(-1, 9 * channels)  23.2 us
    pallas_call x1, Pallas kernels, forward_call(): pl.pallas_call(forward_kernel, out_shape=(wide, wide, low, low, low, jax....  22 us
  transfers between devices with their start and end apart: 17, of which 2 were waited for; matrix products, arithmetic and copies ran while one was open for 58% of the time, Pallas kernels for 0%

profile of v1, /device:TPU:0, one launch (start us, length us, event | category | flops | bytes accessed | tf_op | source)
XLA Modules:
  0.0 551.7 jit_solution(9965398399949185904)
XLA Ops:
  18.2 22.0 %forward.1 = (f32[3,256,384]{2,1,0:T(8,128)}, f32[3,256,384]{2,1,0:T(8,128)}, bf16[3,256,384]{2,1,0:T(8,128)(2,1)}, bf16[3,256,384]{2,1,0:T(8,128)(2,1)}, bf16[3...) custom-call(bf16[3,256,384]{2,1,0:T(8,128)(2,1)} %bitcast.178, f32[8,384]{1,0:T(8,128)} %convert_element_type.166.vec_ref, ...), custom_call_target="tpu_custom_call" | custom-call | tf_op jit(solution)/shard_map/forward/pallas_call | solution.py:308
  53.1 4.1 collective-permute-start.6
  57.2 12.2 %all-reduce.4 = s32[24]{0:T(128)} all-reduce(s32[24]{0:T(128)S(1)} %dynamic-update-slice), channel_id=1, replica_groups=mesh['img'=8,'row'=4] {'img'}, use_global_device_ids=true, to_apply=%add.4 | all-reduce | flops 24 | bytes 192
  77.8 4.4 copy.62
  82.2 9.6 %multiply_reduce_fusion.1 = (f32[3,6,256]{2,1,0:T(8,128)S(1)}, f32[3,6,256,1024]{3,2,1,0:T(8,128)}) fusion(bf16[3,256,6,64]{1,3,2,0:T(8,128)(2,1)S(1)} %bitcast.166, bf16[3,1024,6,64]{1,3,2,0:T(8,128)(2,1)} %bitcast.134), kind=kOutput, calls=%fused_computation.6 | convolution fusion | flops 613412352 | bytes 21841920 | tf_op jit(solution)/shard_map/iphd,ikhd->ihpk/dot_general | solution.py:422
  91.8 9.8 %fusion = f32[3,6,256]{2,1,0:T(8,128)S(1)} fusion(f32[3,6,256,1024]{3,2,1,0:T(8,128)} %get-tuple-element.94, f32[3,6,256]{2,1,0:T(8,128)S(1)} %get-tuple-element.93), kind=kLoop, calls=%fused_computation.5 | loop fusion | flops 14151168 | bytes 18911232 | tf_op jit(solution)/shard_map/reduce_sum | solution.py:427
  101.7 4.3 copy.60
  106.0 13.5 %multiply_reduce_fusion = (f32[3,6,256]{2,1,0:T(8,128)S(1)}, f32[3,6,256,1024]{3,2,1,0:T(8,128)}) fusion(f32[3,6,256,1024]{3,2,1,0:T(8,128)} %get-tuple-element.94, f32[3,6,256]{2,1,0:T(8,128)S(1)} %log_add_fusion, bf16[3,256,6,64]{1,3,2,0:T(8,128)(2,1)S(1)} %copy.65, bf16[3,1024,6,64]{1,3,2,0:T(8,128)(2,1)} %bitcast.164), kind=kOutput, calls=%fused_computation.1 | convolution fusion | flops 622849536 | bytes 40734720 | tf_op jit(solution)/shard_map/iphd,ikhd->ihpk/dot_general | solution.py:460
  119.5 13.0 %multiply_convert_fusion = bf16[3,6,256,1024]{3,2,1,0:T(8,128)(2,1)S(1)} fusion(f32[3,6,256,1024]{3,2,1,0:T(8,128)} %get-tuple-element.96, f32[3,6,256,1024]{3,2,1,0:T(8,128)} %get-tuple-element.94, f32[3,6,256]{2,1,0:T(8,128)S(1)} %get-tuple-element.95, f32[3,6,256]{2,1,0:T(8,128)S(1)} %log_add_fusion), kind=kLoop, calls=%fused_computation | loop fusion | flops 23592960 | bytes 47222784 | tf_op jit(solution)/shard_map/convert_element_type | solution.py:464
  132.6 3.7 copy-done.2
  139.5 30.5 %all-gather = f32[8,3,768]{2,1,0:T(4,128)S(1)} all-gather(f32[1,3,768]{2,1,0:T(4,128)S(1)} %bitcast.186), channel_id=1, replica_groups=mesh['img'=8,'row'=4] {'img'}, dimensions={0}, use_global_device_ids=true | all-gather | bytes 82944 | tf_op jit(solution)/shard_map/all_gather | solution.py:541
  182.0 10.1 %convert_bitcast_fusion = bf16[3,1024,6,64]{1,3,2,0:T(8,128)(2,1)} fusion(bf16[3,256,6,64]{1,3,2,0:T(8,128)(2,1)S(1)} %copy-done.13, f32[3,6,256,1024]{3,2,1,0:T(8,128)} %get-tuple-element.94, f32[3,6,256]{2,1,0:T(8,128)S(1)} %log_add_fusion), kind=kOutput, calls=%fused_computation.25 | convolution fusion | flops 619315200 | bytes 21841920 | tf_op jit(solution)/shard_map/ihpk,iphd->ikhd/dot_general | solution.py:457
  193.6 11.7 %reshape_reshape.9 = bf16[768,9,384]{2,1,0:T(8,128)(2,1)} reshape(bf16[3,8,32,3456]{3,2,1,0:T(8,128)(2,1)} %slice_dynamic-update-slice_fusion) | data formatting | bytes 10616832 | tf_op jit(solution)/shard_map/reshape;reshape | solution.py:400
  205.2 23.8 %rev.7 = bf16[768,9,384]{2,1,0:T(8,128)(2,1)} reverse(bf16[768,9,384]{2,1,0:T(8,128)(2,1)} %reshape_reshape.9), dimensions={1} | reverse | bytes 10616832 | tf_op jit(solution)/shard_map/rev | solution.py:400
  229.1 12.3 %copy.73 = bf16[768,9,384]{0,2,1:T(8,128)(2,1)} copy(bf16[768,9,384]{2,1,0:T(8,128)(2,1)} %rev.7) | data formatting | bytes 10616832 | tf_op jit(solution)/shard_map/rev | solution.py:400
  246.3 9.1 %fusion.33 = bf16[3,256,6,64]{1,3,2,0:T(8,128)(2,1)S(1)} fusion(bf16[3,1024,6,64]{1,3,2,0:T(8,128)(2,1)S(1)} %bitcast.165, f32[3,6,256,1024]{3,2,1,0:T(8,128)} %get-tuple-element.94, f32[3,6,256]{2,1,0:T(8,128)S(1)} %copy-done.27, f32[3,6,256]{2,1,0:T(8,128)S(1)} %get-tuple-element.93), kind=kOutput, calls=%fused_computation.39 | convolution fusion | flops 623149056 | bytes 21860352 | tf_op jit(solution)/shard_map/ihpk,ikhd->iphd/dot_general | solution.py:431
  271.5 3.6 fusion.73
  277.4 5.8 %all-reduce.7 = (f32[3,32]{1,0:T(4,128)S(1)}, f32[3,32]{1,0:T(4,128)S(1)}) all-reduce(f32[3,32]{1,0:T(4,128)S(1)} %reduce_sum.257, f32[3,32]{1,0:T(4,128)S(1)} %reduce_sum.255), channel_id=1, replica_groups=mesh['img'=8,'row'=4] {'row'}, use_global_device_ids=true, to_apply=%region_10.11 | all-reduce | flops 192 | bytes 1536 | tf_op jit(solution)/shard_map/psum | solution.py:55
  286.0 7.0 %convolution_convert_fusion = bf16[3456,384]{1,0:T(8,128)(2,1)} fusion(bf16[768,3456]{0,1:T(8,128)(2,1)} %bitcast.168, bf16[768,384]{1,0:T(8,128)(2,1)S(1)} %bitcast.143), kind=kOutput, calls=%fused_computation.12 | convolution fusion | flops 2039758848 | bytes 8552448 | tf_op jit(solution)/shard_map/dot_general | solution.py:511
  302.0 11.6 %reshape_reshape.8 = bf16[768,9,384]{2,1,0:T(8,128)(2,1)} reshape(bf16[3,8,32,3456]{3,2,1,0:T(8,128)(2,1)} %slice_dynamic-update-slice_fusion.6) | data formatting | bytes 10616832 | tf_op jit(solution)/shard_map/reshape;reshape | solution.py:400
  313.6 23.9 %rev.6 = bf16[768,9,384]{2,1,0:T(8,128)(2,1)} reverse(bf16[768,9,384]{2,1,0:T(8,128)(2,1)} %reshape_reshape.8), dimensions={1} | reverse | bytes 10616832 | tf_op jit(solution)/shard_map/rev | solution.py:400
  337.5 12.4 %copy.72 = bf16[768,9,384]{0,2,1:T(8,128)(2,1)} copy(bf16[768,9,384]{2,1,0:T(8,128)(2,1)} %rev.6) | data formatting | bytes 10616832 | tf_op jit(solution)/shard_map/rev | solution.py:400
  359.2 11.7 %dot_general.80 = bf16[3,256,9,384]{3,2,1,0:T(8,128)(2,1)} reshape(bf16[3,8,32,3456]{3,2,1,0:T(8,128)(2,1)} %slice_dynamic-update-slice_fusion.18) | data formatting | bytes 10616832 | tf_op jit(solution)/shard_map/dot_general | solution.py:91
  370.9 9.3 %multiply_reduce_fusion.4 = (f32[384]{0:T(512)S(1)}, f32[3,384]{1,0:T(4,128)S(1)}, f32[3,384]{1,0:T(4,128)S(1)}, f32[3,384]{1,0:T(4,128)S(1)}, f32[384]{0:T(512)...) fusion(f32[3,256,384]{2,1,0:T(8,128)S(1)} %copy-done.21, f32[3,384]{1,0:T(4,128)S(1)} %copy-done.31, ...), kind=kOutput, calls=%fused_computation.48 | convolution fusion | flops 2045799168 | bytes 10364928 | tf_op jit(solution)/shard_map/dot_general | solution.py:91
  380.6 6.9 %all-reduce.6 = (f32[3,32]{1,0:T(4,128)S(1)}, f32[3,32]{1,0:T(4,128)S(1)}) all-reduce(f32[3,32]{1,0:T(4,128)S(1)} %reduce_sum.261, f32[3,32]{1,0:T(4,128)S(1)} %reduce_sum.259), channel_id=1, replica_groups=mesh['img'=8,'row'=4] {'row'}, use_global_device_ids=true, to_apply=%region_16.17 | all-reduce | flops 192 | bytes 1536 | tf_op jit(solution)/shard_map/psum | solution.py:55
  390.0 6.9 %convolution_convert_fusion.1 = bf16[3456,384]{1,0:T(8,128)(2,1)} fusion(bf16[768,3456]{0,1:T(8,128)(2,1)} %bitcast.169, bf16[768,384]{1,0:T(8,128)(2,1)S(1)} %bitcast.137), kind=kOutput, calls=%fused_computation.13 | convolution fusion | flops 2039758848 | bytes 8552448 | tf_op jit(solution)/shard_map/dot_general | solution.py:528
  414.4 11.6 %dot_general.82 = bf16[3,256,9,384]{3,2,1,0:T(8,128)(2,1)} reshape(bf16[3,8,32,3456]{3,2,1,0:T(8,128)(2,1)} %slice_dynamic-update-slice_fusion.12) | data formatting | bytes 10616832 | tf_op jit(solution)/shard_map/dot_general | solution.py:91
  426.1 9.2 %multiply_reduce_fusion.5 = (f32[384]{0:T(512)S(1)}, f32[3,384]{1,0:T(4,128)S(1)}, f32[3,384]{1,0:T(4,128)S(1)}, f32[384]{0:T(512)S(1)}, f32[3,256,384]{2,1,0:T(8,128)}) fusion(f32[3,384]{1,0:T(4,128)S(1)} %copy-done.29, f32[3,384]{1,0:T(4,128)S(1)} %copy-done.30, bf16[3,8,32,384]{3,2,1,0:T(8,128)(2,1)S(1)} %copy-done.17, f32[384]{0:T(512)S(1)} %copy-done.36, ...), kind=kOutput, calls=%fused_computation.50 | convolution fusion | flops 2045211648 | bytes 10346496 | tf_op jit(solution)/shard_map/dot_general | solution.py:91
  435.7 11.9 %all-reduce.5 = (f32[3,32]{1,0:T(4,128)S(1)}, f32[3,32]{1,0:T(4,128)S(1)}, f32[3,768]{1,0:T(4,128)S(1)}) all-reduce(f32[3,32]{1,0:T(4,128)S(1)} %reduce_sum.265, f32[3,32]{1,0:T(4,128)S(1)} %reduce_sum.263, f32[3,768]{1,0:T(4,128)S(1)} %pad_maximum_fusion.8), channel_id=1, replica_groups=mesh['img'=8,'row'=4] {'row'}, use_global_device_ids=true, to_apply=%region_22.23 | all-reduce | flops 2496 | bytes 19968 | tf_op jit(solution)/shard_map/psum | solution.py:55
  447.9 31.5 %all-gather.1 = f32[8,3,768]{2,1,0:T(4,128)S(1)} all-gather(f32[1,3,768]{2,1,0:T(4,128)S(1)} %bitcast.187), channel_id=1, replica_groups=mesh['img'=8,'row'=4] {'img'}, dimensions={0}, use_global_device_ids=true | all-gather | bytes 82944 | tf_op jit(solution)/shard_map/all_gather | solution.py:541
  479.9 38.7 %psum.90 = f32[4224]{0:T(1024)S(1)} all-reduce(f32[4224]{0:T(1024)S(1)} %constant_dynamic-update-slice_fusion.16), channel_id=1, replica_groups=mesh['img'=8,'row'=4] {'img','row'}, use_global_device_ids=true, to_apply=%region_34.35 | all-reduce | flops 4224 | bytes 33792 | tf_op jit(solution)/shard_map/psum | solution.py:579
  534.0 5.9 %all-reduce.11.cloned.1.call-done = (bf16[864,384]{1,0:T(8,128)(2,1)}, bf16[864,384]{1,0:T(8,128)(2,1)}, bf16[96,1152]{1,0:T(8,128)(2,1)}, bf16[96,384]{1,0:T(8,128)(2,1)}) async-done(((bf16[864,384]{1,0:T(8,128)(2,1)}, bf16[864,384]{1,0:T(8,128)(2,1)}, bf16[96,1152]{1,0:T(8,128)(2,1)}, bf16[96,384]{1,0:T(8,128)(2,1)}), (bf16[864,384]{1,0:T(8,128)(2,1)}, bf16[864,384]{1,0:T(8,128)(2,1)}, ...) | async-done | bytes 1622032 | tf_op jit(solution)/shard_map/psum | solution.py:568
  (341 shorter events, 133.6 us)
Async XLA Ops:
  7.2 70.5 %all-gather.7.cloned.1.call-start = ((), (), s32[]{:S(2)}) async-start(), calls=%async_computation.7 | async-start | bytes 2949120 | tf_op jit(solution)/shard_map/all_gather | solution.py:415
  18.2 22.0 %copy-start.56 = (bf16[384,1152]{1,0:T(8,128)(2,1)S(1)}, bf16[384,1152]{1,0:T(8,128)(2,1)}, u32[]{:S(2)}) copy-start(bf16[384,1152]{1,0:T(8,128)(2,1)} %param.39) | copy-start | bytes 2654212
  42.5 26.9 %copy-start.43 = (bf16[384]{0:T(512)(128)(2,1)S(1)}, bf16[384]{0:T(512)(128)(2,1)}, u32[]{:S(2)}) copy-start(bf16[384]{0:T(512)(128)(2,1)} %param.26) | copy-start | bytes 2308
  42.5 27.5 %copy-start.44 = (bf16[384]{0:T(512)(128)(2,1)S(1)}, bf16[384]{0:T(512)(128)(2,1)}, u32[]{:S(2)}) copy-start(bf16[384]{0:T(512)(128)(2,1)} %param.27) | copy-start | bytes 2308
  42.5 28.1 %copy-start.45 = (bf16[384]{0:T(512)(128)(2,1)S(1)}, bf16[384]{0:T(512)(128)(2,1)}, u32[]{:S(2)}) copy-start(bf16[384]{0:T(512)(128)(2,1)} %param.33) | copy-start | bytes 2308
  42.5 28.7 %copy-start.46 = (bf16[384]{0:T(512)(128)(2,1)S(1)}, bf16[384]{0:T(512)(128)(2,1)}, u32[]{:S(2)}) copy-start(bf16[384]{0:T(512)(128)(2,1)} %param.34) | copy-start | bytes 2308
  42.5 29.3 %copy-start.47 = (bf16[384]{0:T(512)(128)(2,1)S(1)}, bf16[384]{0:T(512)(128)(2,1)}, u32[]{:S(2)}) copy-start(bf16[384]{0:T(512)(128)(2,1)} %param.37) | copy-start | bytes 2308
  43.8 28.3 %copy-start.53 = (bf16[384]{0:T(512)(128)(2,1)S(1)}, bf16[384]{0:T(512)(128)(2,1)}, u32[]{:S(2)}) copy-start(bf16[384]{0:T(512)(128)(2,1)} %param.42) | copy-start | bytes 2308
  43.8 28.9 %copy-start.5 = (bf16[3,8,32,384]{3,2,1,0:T(8,128)(2,1)S(1)}, bf16[3,8,32,384]{3,2,1,0:T(8,128)(2,1)}, u32[]{:S(2)}) copy-start(bf16[3,8,32,384]{3,2,1,0:T(8,128)(2,1)} %param.43) | copy-start | bytes 1769476
  43.8 28.9 %copy-start.19 = (bf16[384,384]{1,0:T(8,128)(2,1)S(1)}, bf16[384,384]{1,0:T(8,128)(2,1)}, u32[]{:S(2)}) copy-start(bf16[384,384]{1,0:T(8,128)(2,1)} %param.41) | copy-start | bytes 884740
  43.8 57.9 %all-gather.5.cloned.1.call-start = ((), (), s32[]{:S(2)}) async-start(), calls=%async_computation.6 | async-start | bytes 2949120 | tf_op jit(solution)/shard_map/all_gather | solution.py:416
  44.5 218.3 %reduce-scatter.7.cloned.1.call-start = ((), (), s32[]{:S(2)}) async-start(), calls=%async_computation.8 | async-start | bytes 2949120 | tf_op jit(solution)/shard_map/reduce_scatter | solution.py:474
  45.3 132.9 %collective-permute-start.5 = (bf16[3,1,32,384]{3,2,1,0:T(8,128)(2,1)}, bf16[3,1,32,384]{3,2,1,0:T(8,128)(2,1)S(1)}, u32[]{:S(2)}, u32[]{:S(2)}) collective-permute-start(bf16[3,1,32,384]{3,2,1,0:T(8,128)(2,1)} %get-tuple-element.67), channel_id=1, source_target_pairs={{1,0},{2,1},{3,2},{5,4},{6,5},{7,6},{9,8},{10,9},{11,10},{13,12},{... | collective-permute-start | bytes 221192 | tf_op jit(solution)/shard_map/ppermute | solution.py:70
  46.6 133.9 %collective-permute-start.4 = (bf16[3,1,32,384]{3,2,1,0:T(8,128)(2,1)}, bf16[3,1,32,384]{3,2,1,0:T(8,128)(2,1)S(1)}, u32[]{:S(2)}, u32[]{:S(2)}) collective-permute-start(bf16[3,1,32,384]{3,2,1,0:T(8,128)(2,1)} %get-tuple-element.66), channel_id=1, source_target_pairs={{0,1},{1,2},{2,3},{4,5},{5,6},{6,7},{8,9},{9,10},{10,11},{12,13},{... | collective-permute-start | bytes 221192 | tf_op jit(solution)/shard_map/ppermute | solution.py:69
  50.3 123.5 %collective-permute-start.7 = (bf16[3,1,32,384]{3,2,1,0:T(8,128)(2,1)}, bf16[3,1,32,384]{3,2,1,0:T(8,128)(2,1)}, u32[]{:S(2)}, u32[]{:S(2)}) collective-permute-start(bf16[3,1,32,384]{3,2,1,0:T(8,128)(2,1)} %get-tuple-element.65), channel_id=1, source_target_pairs={{1,0},{2,1},{3,2},{5,4},{6,5},{7,6},{9,8},{10,9},{11,10},{13,12},{... | collective-permute-start | bytes 221192 | tf_op jit(solution)/shard_map/ppermute | solution.py:70
  53.1 120.7 %collective-permute-start.6 = (bf16[3,1,32,384]{3,2,1,0:T(8,128)(2,1)}, bf16[3,1,32,384]{3,2,1,0:T(8,128)(2,1)}, u32[]{:S(2)}, u32[]{:S(2)}) collective-permute-start(bf16[3,1,32,384]{3,2,1,0:T(8,128)(2,1)} %get-tuple-element.64), channel_id=1, source_target_pairs={{0,1},{1,2},{2,3},{4,5},{5,6},{6,7},{8,9},{9,10},{10,11},{12,13},{... | collective-permute-start | bytes 221192 | tf_op jit(solution)/shard_map/ppermute | solution.py:69
  77.0 29.0 %copy-start.12 = (bf16[3,256,6,64]{1,3,2,0:T(8,128)(2,1)}, bf16[3,256,6,64]{1,3,2,0:T(8,128)(2,1)S(1)}, u32[]{:S(2)}) copy-start(bf16[3,256,6,64]{1,3,2,0:T(8,128)(2,1)S(1)} %copy.65) | copy-start | bytes 1769476
  139.4 31.3 %copy-start.34 = (f32[3,8,384]{2,1,0:T(8,128)S(1)}, f32[3,8,384]{2,1,0:T(8,128)}, u32[]{:S(2)}) copy-start(f32[3,8,384]{2,1,0:T(8,128)} %get-tuple-element.27) | copy-start | bytes 110596
  139.4 125.1 %reduce-scatter.9.cloned.1.call-start = ((), (), s32[]{:S(2)}) async-start(), calls=%async_computation.9 | async-start | bytes 2949120 | tf_op jit(solution)/shard_map/reduce_scatter | solution.py:477
  192.2 255.6 %reduce-scatter.17.cloned.1.call-start = ((), (), s32[]{:S(2)}) async-start(), calls=%async_computation.13 | async-start | bytes 368640 | tf_op jit(solution)/shard_map/reduce_scatter | solution.py:567
  261.9 185.9 %reduce-scatter.15.cloned.1.call-start = ((), (), s32[]{:S(2)}) async-start(), calls=%async_computation.12 | async-start | bytes 1105920 | tf_op jit(solution)/shard_map/reduce_scatter | solution.py:567
  271.5 176.3 %reduce-scatter.13.cloned.1.call-start = ((), (), s32[]{:S(2)}) async-start(), calls=%async_computation.11 | async-start | bytes 3317760 | tf_op jit(solution)/shard_map/reduce_scatter | solution.py:567
  293.0 154.8 %reduce-scatter.11.cloned.1.call-start = ((), (), s32[]{:S(2)}) async-start(), calls=%async_computation.10 | async-start | bytes 3317760 | tf_op jit(solution)/shard_map/reduce_scatter | solution.py:567
  296.8 53.2 %collective-permute-start.1 = (bf16[3,1,32,384]{3,2,1,0:T(8,128)(2,1)}, bf16[3,1,32,384]{3,2,1,0:T(8,128)(2,1)S(1)}, u32[]{:S(2)}, u32[]{:S(2)}) collective-permute-start(bf16[3,1,32,384]{3,2,1,0:T(8,128)(2,1)} %get-tuple-element.71), channel_id=1, source_target_pairs={{1,0},{2,1},{3,2},{5,4},{6,5},{7,6},{9,8},{10,9},{11,10},{13,12},{... | collective-permute-start | bytes 221192 | tf_op jit(solution)/shard_map/ppermute | solution.py:70
  298.1 51.9 %collective-permute-start = (bf16[3,1,32,384]{3,2,1,0:T(8,128)(2,1)}, bf16[3,1,32,384]{3,2,1,0:T(8,128)(2,1)S(1)}, u32[]{:S(2)}, u32[]{:S(2)}) collective-permute-start(bf16[3,1,32,384]{3,2,1,0:T(8,128)(2,1)} %get-tuple-element.70), channel_id=1, source_target_pairs={{0,1},{1,2},{2,3},{4,5},{5,6},{6,7},{8,9},{9,10},{10,11},{12,13},{... | collective-permute-start | bytes 221192 | tf_op jit(solution)/shard_map/ppermute | solution.py:69
  396.9 143.0 %all-reduce.11.cloned.1.call-start = ((), (), s32[]{:S(2)}) async-start(), calls=%async_computation.14 | async-start | bytes 3244032 | tf_op jit(solution)/shard_map/psum | solution.py:568
  399.9 4.4 collective-permute-start.3
  401.2 3.9 collective-permute-start.2
  435.3 44.6 %copy-start.37 = (f32[384]{0:T(512)S(1)}, f32[384]{0:T(512)}, u32[]{:S(2)}) copy-start(f32[384]{0:T(512)} %convert_reduce_fusion.2) | copy-start | bytes 4612
  447.9 81.8 %copy-start.52 = (s32[250]{0:T(256)S(1)}, s32[250]{0:T(256)}, u32[]{:S(2)}) copy-start(s32[250]{0:T(256)} %iota_add_fusion) | copy-start | bytes 3004
  447.9 81.7 %copy-start.55 = (s32[24]{0:T(128)S(1)}, s32[24]{0:T(128)}, u32[]{:S(2)}) copy-start(s32[24]{0:T(128)} %all-reduce.4) | copy-start | bytes 292
  447.9 83.2 %copy-start.9 = (f32[768,384]{1,0:T(8,128)S(1)}, f32[768,384]{1,0:T(8,128)}, u32[]{:S(2)}) copy-start(f32[768,384]{1,0:T(8,128)} %copy-done.8) | copy-start | bytes 3538948
  (47 other events, 381.2 us)
Sparse Core Ops, SparseCore 0:
  43.9 25.7 all-gather.6
  71.9 24.0 all-gather.4
  139.6 30.8 reduce-scatter.6
  192.3 30.7 reduce-scatter.8
  262.0 18.0 reduce-scatter.16
  283.3 24.6 reduce-scatter.14
  310.6 34.8 reduce-scatter.12
  397.0 33.4 reduce-scatter.10
  448.0 91.8 all-reduce.10
